TPU v7x, 32 devices: a whole 2x2x4 slice. The times are simulated.
32 devices in a mesh: gx: 8 (over z, y), gy: 2 (over x), gz: 2 (over core).
Axes of the slice: x: 2, y: 2, z: 4, core: 2. Of those that a mesh axis runs over, the one named last changes fastest.
Arguments:
- pops: float32 [19, 32, 64, 256], P(None, 'gz', 'gx', 'gy'), as said below
- solid: int32 [32, 64, 256], P('gz', 'gx', 'gy'), may hold values 0 or 1
- surf_cell: int32 [2, 8, 2, 512], P('gz', 'gx', 'gy'), may hold values from 0 to 16383
- surf_panel: int32 [2, 8, 2, 512], P('gz', 'gx', 'gy'), may hold values from -1 to 39, as said below
- surf_area: float32 [2, 8, 2, 512], P('gz', 'gx', 'gy'), may hold values from 0.1 to 1
- mode_shape: float32 [2, 8, 2, 12, 512], P('gz', 'gx', 'gy'), may hold values from -5 to 5
- mode_of_panel: int32 [40], replicated, may hold values from 0 to 11
- compliance: float32 [12], replicated, may hold values from 0.3 to 3
Outputs:
- read: float32 [19, 32, 64, 256], P(None, 'gz', 'gx', 'gy')
- panel_force: float32 [40], replicated
- mode_amplitude: float32 [12], replicated
Inputs may be any that keep to these rules, and one draw needn't show every extreme that they name: pops is positive, with densities near 1 and flow speeds below 0.25. `surf_panel`: -1 marks an empty slot; on each device the live slots come first, at least 64 of them; some device has all 512 slots live; one panel's surfels lie on at most about 40 consecutive bricks in the linear order (vertical, streamwise, crosswise) of the devices, counted periodically so that the last brick is followed by the first.
All inputs are finite; a program needn't handle non-finite values. No bound on the sum of `solid` on one device may be relied on, other than what follows from the above.
Results may differ from a plain program's by a relative error of at most 0.00011.
Values sent between devices are 32-bit elements; how exact they have to be, the bound alone decides.
A program may use at most 64 MiB of HBM per device.

v0:
```python
import jax
import jax.numpy as jnp
from jax import lax
from jax.sharding import PartitionSpec as P

PANELS = 40
MODES = 12
VELOCITY = (
    (0, 0, 0),
    (1, 0, 0),
    (-1, 0, 0),
    (0, 1, 0),
    (0, -1, 0),
    (0, 0, 1),
    (0, 0, -1),
    (1, 1, 0),
    (-1, -1, 0),
    (1, -1, 0),
    (-1, 1, 0),
    (1, 0, 1),
    (-1, 0, -1),
    (1, 0, -1),
    (-1, 0, 1),
    (0, 1, 1),
    (0, -1, -1),
    (0, 1, -1),
    (0, -1, 1),
)
WEIGHTS = (1.0 / 3.0,) + (1.0 / 18.0,) * 6 + (1.0 / 36.0,) * 12
OPPOSITE = (0, 2, 1, 4, 3, 6, 5, 8, 7, 10, 9, 12, 11, 14, 13, 16, 15, 18, 17)
OMEGA = 1.0 / 0.6
WALL_SCALE = 0.02


def padded_2(block, sides, width):
    for axis, dim in sides:
        count = lax.axis_size(axis)
        forward = [(i, i + 1) for i in range(count - 1)]
        forward.append((count - 1, 0))
        backward = [(target, source) for source, target in forward]
        low = lax.ppermute(
            lax.slice_in_dim(block, block.shape[dim] - width, None, axis=dim), axis, forward
        )
        high = lax.ppermute(lax.slice_in_dim(block, 0, width, axis=dim), axis, backward)
        block = jnp.concatenate([low, block, high], axis=dim)
    return block


def collide(pops, solid):
    density = pops[0]
    for index in range(1, 19):
        density = density + pops[index]
    moments = []
    for axis in range(3):
        total = jnp.zeros_like(density)
        for index in range(19):
            comp = VELOCITY[index][axis]
            if comp == 1:
                total = total + pops[index]
            elif comp == -1:
                total = total - pops[index]
        moments.append(total / density)
    squared = moments[0] * moments[0] + moments[1] * moments[1] + moments[2] * moments[2]
    result = []
    for index in range(19):
        projected = jnp.zeros_like(density)
        for axis in range(3):
            comp = VELOCITY[index][axis]
            if comp == 1:
                projected = projected + moments[axis]
            elif comp == -1:
                projected = projected - moments[axis]
        equilib = (
            WEIGHTS[index]
            * density
            * (1.0 + 3.0 * projected + 4.5 * projected * projected - 1.5 * squared)
        )
        relaxed = pops[index] + OMEGA * (equilib - pops[index])
        result.append(jnp.where(solid == 1, pops[OPPOSITE[index]], relaxed))
    return (density, result)


def stream_joint(pieces):
    field = jnp.stack(pieces)
    depth, rows, width = (field.shape[1], field.shape[2], field.shape[3])
    padded = padded_2(field, (("gx", 2), ("gy", 3), ("gz", 1)), 1)
    result = []
    for index in range(19):
        vel = VELOCITY[index]
        result.append(
            padded[
                index,
                1 - vel[2] : 1 - vel[2] + depth,
                1 - vel[0] : 1 - vel[0] + rows,
                1 - vel[1] : 1 - vel[1] + width,
            ]
        )
    return result


def stream_all(pieces):
    return stream_joint(pieces)


def per_device(
    pops, solid, surf_cell, surf_panel, surf_area, mode_shape, mode_of_panel, compliance
):
    depth, rows, width = (pops.shape[1], pops.shape[2], pops.shape[3])
    density, post = collide(pops, solid)
    flat_density = density.reshape(-1)
    cell_list = surf_cell.reshape(-1)
    panel_list = surf_panel.reshape(-1)
    gathered = flat_density[cell_list]
    live = panel_list >= 0
    contrib = jnp.where(live, surf_area.reshape(-1) * ((gathered - 1.0) / 3.0), 0.0)
    panel_ids = jnp.arange(PANELS, dtype=jnp.int32)
    partial_force = jnp.sum(
        jnp.where(panel_list[:, None] == panel_ids[None, :], contrib[:, None], 0.0), axis=0
    )
    panel_force = lax.psum(partial_force, ("gx", "gy", "gz"))
    mode_ids = jnp.arange(MODES, dtype=jnp.int32)
    mode_load = jnp.sum(
        jnp.where(mode_of_panel[:, None] == mode_ids[None, :], panel_force[:, None], 0.0), axis=0
    )
    mode_amplitude = compliance * mode_load
    shapes = mode_shape.reshape(MODES, -1)
    wall = WALL_SCALE * jnp.sum(mode_amplitude[:, None] * shapes, axis=0)
    values = jnp.where(live, gathered * wall, 0.0)
    wall_flux = jnp.zeros_like(flat_density).at[cell_list].add(values).reshape(depth, rows, width)
    corrected = []
    for index in range(19):
        coef = 6.0 * WEIGHTS[index] * VELOCITY[index][0]
        corrected.append(post[index] + coef * wall_flux)
    result = stream_all(corrected)
    return (jnp.stack(result), panel_force, mode_amplitude)


def solution(mesh):
    placed = (
        P(None, "gz", "gx", "gy"),
        P("gz", "gx", "gy"),
        P("gz", "gx", "gy", None),
        P("gz", "gx", "gy", None),
        P("gz", "gx", "gy", None),
        P("gz", "gx", "gy", None, None),
        P(),
        P(),
    )
    return jax.shard_map(
        per_device,
        mesh=mesh,
        in_specs=placed,
        out_specs=(P(None, "gz", "gx", "gy"), P(), P()),
        check_vma=False,
    )
```

profile of v0, /device:TPU:0, one launch (start us, length us, event | category | flops | bytes accessed | tf_op | source)
XLA Modules:
  0.0 97.8 jit_solution(2532107182724770170)
XLA Ops:
  0.6 0.7 compare_select_fusion
  1.3 1.4 %bitcast_add_fusion = f32[16384]{0:T(1024)S(1)} fusion(f32[19,16,8,128]{3,2,1,0:T(8,128)} %param.8), kind=kLoop, calls=%fused_computation.249 | loop fusion | flops 294912 | bytes 1310720 | tf_op jit(solution)/shard_map/add | solution.py:52
  2.7 0.0 copy-start.7
  2.7 0.0 copy-start.9
  2.8 0.0 copy-start.2
  2.8 3.1 %gather_fusion = f32[512]{0:T(512)S(1)} fusion(f32[16384]{0:T(1024)S(1)} %bitcast_add_fusion, s32[1024]{0:T(1024)S(1)} %pad_clamp_fusion), kind=kCustom, calls=%fused_computation | custom fusion | bytes 6144 | tf_op jit(solution)/shard_map/gather | solution.py:113
  6.0 0.1 select_reduce_fusion
  6.1 42.0 %psum.7 = f32[40]{0:T(128)S(1)} all-reduce(f32[40]{0:T(128)S(1)} %select_reduce_fusion), channel_id=1, replica_groups=mesh['gx'=8,'gy'=2,'gz'=2] {'gx','gy','gz'}, use_global_device_ids=true, to_apply=%region_1.2 | all-reduce | flops 40 | bytes 320 | tf_op jit(solution)/shard_map/psum | solution.py:120
  48.1 0.1 select_reduce_fusion.1
  48.2 0.0 copy-start.8
  48.3 0.1 fusion.168
  48.4 3.3 %scatter_custom_fusion = f32[16384]{0:T(1024)S(1)} fusion(s32[512]{0:T(512)S(1)} %bitcast.409, f32[512]{0:T(512)S(1)} %multiply_select_fusion, f32[]{:T(128)} %constant.4.clone.1), kind=kCustom, calls=%fused_computation.305 | custom fusion | flops 512 | bytes 65540 | tf_op jit(solution)/shard_map/scatter-add | solution.py:129
  51.7 0.2 fusion.1
  51.9 0.1 copy.82
  52.9 0.2 fusion.175
  53.1 2.3 %collective-permute-start = (f32[19,16,1,128]{3,1,2,0:T(8,128)S(1)}, f32[19,16,1,128]{3,1,2,0:T(8,128)S(1)}, u32[]{:S(2)}, u32[]{:S(2)}) collective-permute-start(f32[19,16,1,128]{3,1,2,0:T(8,128)S(1)} %bitcast.405), channel_id=1, source_target_pairs={{0,4},{4,8},{8,12},{12,16},{16,20},{20,24},{24,28},{28,0},{1,5},{5... | collective-permute-start | bytes 466952 | tf_op jit(solution)/shard_map/ppermute | solution.py:41
  55.4 2.5 %collective-permute-start.1 = (f32[19,16,1,128]{3,1,2,0:T(8,128)S(1)}, f32[19,16,1,128]{3,1,2,0:T(8,128)S(1)}, u32[]{:S(2)}, u32[]{:S(2)}) collective-permute-start(f32[19,16,1,128]{3,1,2,0:T(8,128)S(1)} %bitcast.404), channel_id=1, source_target_pairs={{4,0},{8,4},{12,8},{16,12},{20,16},{24,20},{28,24},{0,28},{5,1},{9... | collective-permute-start | bytes 466952 | tf_op jit(solution)/shard_map/ppermute | solution.py:44
  57.9 3.3 %collective-permute-done = f32[19,16,1,128]{3,1,2,0:T(8,128)S(1)} collective-permute-done((f32[19,16,1,128]{3,1,2,0:T(8,128)S(1)}, f32[19,16,1,128]{3,1,2,0:T(8,128)S(1)}, u32[]{:S(2)}, u32[]{:S(2)}) %collective-permute-start) | collective-permute-done | bytes 155680 | tf_op jit(solution)/shard_map/ppermute | solution.py:41
  61.2 1.3 %collective-permute-done.1 = f32[19,16,1,128]{3,1,2,0:T(8,128)S(1)} collective-permute-done((f32[19,16,1,128]{3,1,2,0:T(8,128)S(1)}, f32[19,16,1,128]{3,1,2,0:T(8,128)S(1)}, u32[]{:S(2)}, u32[]{:S(2)}) %collective-permute-start.1) | collective-permute-done | bytes 155680 | tf_op jit(solution)/shard_map/ppermute | solution.py:44
  62.5 0.5 pad_maximum_fusion
  63.0 3.1 %fusion.174 = (f32[19,16,10,1]{3,2,1,0:T(8,128)}, f32[19,16,10,1]{3,2,1,0:T(8,128)}) fusion(f32[19,16,10,128]{3,2,1,0:T(8,128)S(1)} %pad_maximum_fusion), kind=kLoop, calls=%fused_computation.315 | loop fusion | bytes 48640 | tf_op jit(solution)/shard_map/slice | solution.py:44
  66.1 2.8 %copy.56 = f32[19,16,10,1]{0,1,3,2:T(8,128)S(1)} copy(f32[19,16,10,1]{3,2,1,0:T(8,128)} %get-tuple-element.18) | data formatting | bytes 24320 | tf_op jit(solution)/shard_map/slice | solution.py:42
  68.9 2.1 %collective-permute-start.2 = (f32[19,16,10,1]{0,1,3,2:T(8,128)S(1)}, f32[19,16,10,1]{0,1,3,2:T(8,128)S(1)}, u32[]{:S(2)}, u32[]{:S(2)}) collective-permute-start(f32[19,16,10,1]{0,1,3,2:T(8,128)S(1)} %copy.56), channel_id=1, source_target_pairs={{0,2},{2,0},{1,3},{3,1},{4,6},{6,4},{5,7},{7,5},{8,10},{10,8},{9,1... | collective-permute-start | bytes 36488 | tf_op jit(solution)/shard_map/ppermute | solution.py:41
  71.0 0.6 constant_dynamic-update-slice_fusion.35
  71.6 2.8 %copy.58 = f32[19,16,10,1]{0,1,3,2:T(8,128)S(1)} copy(f32[19,16,10,1]{3,2,1,0:T(8,128)} %get-tuple-element.17) | data formatting | bytes 24320 | tf_op jit(solution)/shard_map/slice | solution.py:44
  74.5 0.1 collective-permute-start.3
  74.5 3.7 %copy.57 = f32[19,16,10,1]{3,2,1,0:T(8,128)} copy(f32[19,16,10,1]{0,1,3,2:T(8,128)S(1)} %collective-permute-done.2) | data formatting | bytes 24320 | tf_op jit(solution)/shard_map/ppermute | solution.py:41
  78.2 1.6 %constant_dynamic-update-slice_fusion.34 = f32[19,16,8,128]{3,2,1,0:T(8,128)} fusion(f32[19,16,8,128]{3,2,1,0:T(8,128)} %constant_dynamic-update-slice_fusion.35, f32[19,16,10,1]{3,2,1,0:T(8,128)} %copy.57, f32[19,16,1,128]{3,2,1,0:T(1,128)S(1)} %bitcast.387, f32[19,16,8,128]{3,2,1,0:T(8,128)S(1)} %constant_dynamic-update-slice_fusion, ...), kind=kLoop, calls=%fused_computation.63 | loop fusion | flops 49152 | bytes 4112384
  79.9 3.7 %copy.59 = f32[19,16,10,1]{3,2,1,0:T(8,128)} copy(f32[19,16,10,1]{0,1,3,2:T(8,128)S(1)} %collective-permute-done.3) | data formatting | bytes 24320 | tf_op jit(solution)/shard_map/ppermute | solution.py:44
  83.6 1.8 %pad_maximum_fusion.1 = (f32[19,1,10,130]{3,2,1,0:T(8,128)S(1)}, f32[19,1,10,130]{3,2,1,0:T(8,128)S(1)}) fusion(f32[19,16,10,1]{3,2,1,0:T(8,128)} %copy.59, f32[19,16,10,1]{3,2,1,0:T(8,128)} %copy.57, f32[19,16,1,128]{3,2,1,0:T(1,128)S(1)} %bitcast.388, f32[19,16,8,128]{3,2,1,0:T(8,128)S(1)} %constant_dynamic-update-slice_fusion, ...), kind=kLoop, calls=%fused_computation.3 | loop fusion | flops 197600 | bytes 1778400 | tf_op jit(solution)/shard_map/concatenate | solution.py:45
  85.4 0.1 collective-permute-start.5
  85.5 0.5 collective-permute-start.4
  85.9 0.8 constant_dynamic-update-slice_fusion.33
  86.7 0.8 collective-permute-done.4
  87.5 0.7 constant_dynamic-update-slice_fusion.32
  88.2 0.7 constant_dynamic-update-slice_fusion.31
  88.9 0.7 constant_dynamic-update-slice_fusion.30
  89.7 0.8 constant_dynamic-update-slice_fusion.29
  90.4 0.8 constant_dynamic-update-slice_fusion.28
  91.2 0.8 constant_dynamic-update-slice_fusion.27
  91.9 0.7 constant_dynamic-update-slice_fusion.26
  92.6 0.7 constant_dynamic-update-slice_fusion.25
  93.4 0.7 constant_dynamic-update-slice_fusion.24
  94.1 0.7 constant_dynamic-update-slice_fusion.23
  94.8 0.7 constant_dynamic-update-slice_fusion.22
  95.5 0.8 constant_dynamic-update-slice_fusion.21
  96.3 0.7 constant_dynamic-update-slice_fusion.20
  97.0 0.8 constant_dynamic-update-slice_fusion.19
  (47 shorter events, 0.9 us)
Async XLA Ops:
  2.7 3.2 %copy-start.6 = (s32[1,1,1,512]{3,2,1,0:T(1,128)S(1)}, s32[1,1,1,512]{3,2,1,0:T(1,128)}, u32[]{:S(2)}) copy-start(s32[1,1,1,512]{3,2,1,0:T(1,128)} %param.11) | copy-start | bytes 6148
  2.7 3.2 %copy-start.7 = (f32[1,1,1,512]{3,2,1,0:T(1,128)S(1)}, f32[1,1,1,512]{3,2,1,0:T(1,128)}, u32[]{:S(2)}) copy-start(f32[1,1,1,512]{3,2,1,0:T(1,128)} %param.12) | copy-start | bytes 6148
  2.7 45.4 %copy-start.9 = (s32[40]{0:T(128)S(1)}, s32[40]{0:T(128)}, u32[]{:S(2)}) copy-start(s32[40]{0:T(128)} %param.14) | copy-start | bytes 484
  2.7 45.5 %copy-start.10 = (f32[12]{0:T(128)S(1)}, f32[12]{0:T(128)}, u32[]{:S(2)}) copy-start(f32[12]{0:T(128)} %param.15) | copy-start | bytes 148
  2.7 45.5 %copy-start.5 = (f32[1,1,1,12,512]{4,2,3,1,0:T(1,128)S(1)}, f32[1,1,1,12,512]{4,2,3,1,0:T(1,128)}, u32[]{:S(2)}) copy-start(f32[1,1,1,12,512]{4,2,3,1,0:T(1,128)} %param.13) | copy-start | bytes 73732
  2.8 48.9 %copy-start.2 = (f32[19,16,8,128]{3,2,1,0:T(8,128)S(1)}, f32[19,16,8,128]{3,2,1,0:T(8,128)}, u32[]{:S(2)}) copy-start(f32[19,16,8,128]{3,2,1,0:T(8,128)} %param.8) | copy-start | bytes 3735556
  2.8 48.9 %copy-start.4 = (s32[16,8,128]{2,1,0:T(8,128)S(1)}, s32[16,8,128]{2,1,0:T(8,128)}, u32[]{:S(2)}) copy-start(s32[16,8,128]{2,1,0:T(8,128)} %param.9) | copy-start | bytes 196612
  48.1 3.9 %copy-start.11 = (f32[40]{0:T(128)}, f32[40]{0:T(128)S(1)}, u32[]{:S(2)}) copy-start(f32[40]{0:T(128)S(1)} %psum.7) | copy-start | bytes 484
  48.2 3.7 %copy-start.8 = (f32[12]{0:T(128)}, f32[12]{0:T(128)S(1)}, u32[]{:S(2)}) copy-start(f32[12]{0:T(128)S(1)} %mul.413) | copy-start | bytes 148
  53.1 8.0 %collective-permute-start = (f32[19,16,1,128]{3,1,2,0:T(8,128)S(1)}, f32[19,16,1,128]{3,1,2,0:T(8,128)S(1)}, u32[]{:S(2)}, u32[]{:S(2)}) collective-permute-start(f32[19,16,1,128]{3,1,2,0:T(8,128)S(1)} %bitcast.405), channel_id=1, source_target_pairs={{0,4},{4,8},{8,12},{12,16},{16,20},{20,24},{24,28},{28,0},{1,5},{5... | collective-permute-start | bytes 466952 | tf_op jit(solution)/shard_map/ppermute | solution.py:41
  55.4 7.1 %collective-permute-start.1 = (f32[19,16,1,128]{3,1,2,0:T(8,128)S(1)}, f32[19,16,1,128]{3,1,2,0:T(8,128)S(1)}, u32[]{:S(2)}, u32[]{:S(2)}) collective-permute-start(f32[19,16,1,128]{3,1,2,0:T(8,128)S(1)} %bitcast.404), channel_id=1, source_target_pairs={{4,0},{8,4},{12,8},{16,12},{20,16},{24,20},{28,24},{0,28},{5,1},{9... | collective-permute-start | bytes 466952 | tf_op jit(solution)/shard_map/ppermute | solution.py:44
  61.2 1.4 %copy-start.3 = (f32[19,16,8,128]{3,2,1,0:T(8,128)}, f32[19,16,8,128]{3,2,1,0:T(8,128)S(1)}, u32[]{:S(2)}) copy-start(f32[19,16,8,128]{3,2,1,0:T(8,128)S(1)} %constant_dynamic-update-slice_fusion.36) | copy-start | bytes 3735556
  68.9 5.6 %collective-permute-start.2 = (f32[19,16,10,1]{0,1,3,2:T(8,128)S(1)}, f32[19,16,10,1]{0,1,3,2:T(8,128)S(1)}, u32[]{:S(2)}, u32[]{:S(2)}) collective-permute-start(f32[19,16,10,1]{0,1,3,2:T(8,128)S(1)} %copy.56), channel_id=1, source_target_pairs={{0,2},{2,0},{1,3},{3,1},{4,6},{6,4},{5,7},{7,5},{8,10},{10,8},{9,1... | collective-permute-start | bytes 36488 | tf_op jit(solution)/shard_map/ppermute | solution.py:41
  74.5 5.4 %collective-permute-start.3 = (f32[19,16,10,1]{0,1,3,2:T(8,128)S(1)}, f32[19,16,10,1]{0,1,3,2:T(8,128)S(1)}, u32[]{:S(2)}, u32[]{:S(2)}) collective-permute-start(f32[19,16,10,1]{0,1,3,2:T(8,128)S(1)} %copy.58), channel_id=1, source_target_pairs={{2,0},{0,2},{3,1},{1,3},{6,4},{4,6},{7,5},{5,7},{10,8},{8,10},{11,... | collective-permute-start | bytes 36488 | tf_op jit(solution)/shard_map/ppermute | solution.py:44
  83.6 2.4 %copy-start.1 = (f32[19,16,10,1]{3,2,1,0:T(8,128)S(1)}, f32[19,16,10,1]{3,2,1,0:T(8,128)}, u32[]{:S(2)}) copy-start(f32[19,16,10,1]{3,2,1,0:T(8,128)} %copy.59) | copy-start | bytes 36484
  85.4 2.8 %collective-permute-start.5 = (f32[19,1,10,130]{3,2,1,0:T(8,128)S(1)}, f32[19,1,10,130]{3,2,1,0:T(8,128)S(1)}, u32[]{:S(2)}, u32[]{:S(2)}) collective-permute-start(f32[19,1,10,130]{3,2,1,0:T(8,128)S(1)} %get-tuple-element.15), channel_id=1, source_target_pairs={{1,0},{0,1},{3,2},{2,3},{5,4},{4,5},{7,6},{6,7},{9,8},{8,9},{11,10... | collective-permute-start | bytes 296408 | tf_op jit(solution)/shard_map/ppermute | solution.py:44
  85.4 2.0 %copy-start = (f32[19,16,10,1]{3,2,1,0:T(8,128)S(1)}, f32[19,16,10,1]{3,2,1,0:T(8,128)}, u32[]{:S(2)}) copy-start(f32[19,16,10,1]{3,2,1,0:T(8,128)} %copy.57) | copy-start | bytes 36484
  85.5 2.0 %collective-permute-start.4 = (f32[19,1,10,130]{3,2,1,0:T(8,128)S(1)}, f32[19,1,10,130]{3,2,1,0:T(8,128)S(1)}, u32[]{:S(2)}, u32[]{:S(2)}) collective-permute-start(f32[19,1,10,130]{3,2,1,0:T(8,128)S(1)} %get-tuple-element.16), channel_id=1, source_target_pairs={{0,1},{1,0},{2,3},{3,2},{4,5},{5,4},{6,7},{7,6},{8,9},{9,8},{10,11... | collective-permute-start | bytes 296408 | tf_op jit(solution)/shard_map/ppermute | solution.py:41
where the time goes:
time: 98.2 us; the launch traced here: 97.8 us
  blocking collectives  42 us (43%)
  other arithmetic  22.3 us (23%)
  local copies, waits for them, and re-layouts  19.7 us (20%)
  starting transfers between devices  7.45 us (8%)
  waiting for transfers between devices  5.39 us (5%)
  between operations  0.99 us (1%)
    psum x1, blocking collectives, per_device(): panel_force = lax.psum(partial_force, ('gx', 'gy', 'gz'))  42 us
    unnamed x34, other arithmetic  13.4 us
    slice x3, local copies, waits for them, and re-layouts, padded_2(): lax.slice_in_dim(block, 0, width, axis=dim)  6.12 us
    ppermute x3, starting transfers between devices, padded_2(): lax.ppermute(lax.slice_in_dim(block, block.shape[dim] - width, None, axis...  4.86 us
    ppermute x3, waiting for transfers between devices, padded_2(): lax.ppermute(lax.slice_in_dim(block, block.shape[dim] - width, None, axis...  4.05 us
    ppermute x1, local copies, waits for them, and re-layouts, padded_2(): lax.ppermute(lax.slice_in_dim(block, block.shape[dim] - width, None, axis...  3.71 us
    ppermute x1, local copies, waits for them, and re-layouts, padded_2(): lax.ppermute(lax.slice_in_dim(block, 0, width, axis=dim), axis, backward)  3.7 us
    scatter-add x1, other arithmetic, per_device(): jnp.zeros_like(flat_density).at[cell_list].add(values)  3.28 us
  transfers between devices with their start and end apart: 6, of which 3 were waited for; matrix products, arithmetic and copies ran while one was open for 11% of the time, Pallas kernels for 0%

commit v1 on v0

--- a/solution.py
+++ b/solution.py
@@ -117,7 +117,7 @@
     partial_force = jnp.sum(
         jnp.where(panel_list[:, None] == panel_ids[None, :], contrib[:, None], 0.0), axis=0
     )
-    panel_force = lax.psum(partial_force, ("gx", "gy", "gz"))
+    panel_force = lax.psum(lax.psum(partial_force, ("gy", "gz")), "gx")
     mode_ids = jnp.arange(MODES, dtype=jnp.int32)
     mode_load = jnp.sum(
         jnp.where(mode_of_panel[:, None] == mode_ids[None, :], panel_force[:, None], 0.0), axis=0

time: 98.2 us -> 85.7 us (0.87)
  blocking collectives: 42 us -> 30 us
  waiting for transfers between devices: 5.39 us -> 4 us
    psum x1 -> x2, blocking collectives: 42 us -> 30 us  [per_device(): panel_force = lax.psum(lax.psum(partial_force, ('gy', 'gz')), 'gx')]
    ppermute x3, starting transfers between devices: 4.86 us -> 1.09 us  [padded_2(): lax.ppermute(lax.slice_in_dim(block, block.shape[dim] - width, None, axis...]
    ppermute x3, starting transfers between devices: 2.58 us -> 6.35 us  [padded_2(): lax.ppermute(lax.slice_in_dim(block, 0, width, axis=dim), axis, backward)]
    ppermute x3, waiting for transfers between devices: 1.34 us -> 0.01 us  [padded_2(): lax.ppermute(lax.slice_in_dim(block, 0, width, axis=dim), axis, backward)]
    unnamed x26, local copies, waits for them, and re-layouts: 0.18 us -> 1.19 us
  transfers between devices with their start and end apart: 6 -> 6, of which waited for: 3 -> 2; matrix products, arithmetic and copies ran while one was open for 11% -> 12% of each run, Pallas kernels for 0% -> 0%
where the time goes in v1:
time: 85.7 us; the launch traced here: 85.4 us
  blocking collectives  30 us (35%)
  other arithmetic  22.3 us (26%)
  local copies, waits for them, and re-layouts  20.6 us (24%)
  starting transfers between devices  7.43 us (9%)
  waiting for transfers between devices  4 us (5%)
  between operations  1 us (1%)
    psum x2, blocking collectives, per_device(): panel_force = lax.psum(lax.psum(partial_force, ('gy', 'gz')), 'gx')  30 us
    unnamed x34, other arithmetic  13.4 us
    ppermute x3, starting transfers between devices, padded_2(): lax.ppermute(lax.slice_in_dim(block, 0, width, axis=dim), axis, backward)  6.35 us
    slice x3, local copies, waits for them, and re-layouts, padded_2(): lax.slice_in_dim(block, 0, width, axis=dim)  6.09 us
    ppermute x3, waiting for transfers between devices, padded_2(): lax.ppermute(lax.slice_in_dim(block, block.shape[dim] - width, None, axis...  3.99 us
    ppermute x1, local copies, waits for them, and re-layouts, padded_2(): lax.ppermute(lax.slice_in_dim(block, 0, width, axis=dim), axis, backward)  3.69 us
    ppermute x1, local copies, waits for them, and re-layouts, padded_2(): lax.ppermute(lax.slice_in_dim(block, block.shape[dim] - width, None, axis...  3.68 us
    scatter-add x1, other arithmetic, per_device(): jnp.zeros_like(flat_density).at[cell_list].add(values)  3.28 us
  transfers between devices with their start and end apart: 6, of which 2 were waited for; matrix products, arithmetic and copies ran while one was open for 12% of the time, Pallas kernels for 0%

profile of v1, /device:TPU:0, one launch (start us, length us, event | category | flops | bytes accessed | tf_op | source)
XLA Modules:
  0.0 85.4 jit_solution(3776098645596406487)
XLA Ops:
  0.6 0.7 compare_select_fusion
  1.3 1.4 %bitcast_add_fusion = f32[16384]{0:T(1024)S(1)} fusion(f32[19,16,8,128]{3,2,1,0:T(8,128)} %param.8), kind=kLoop, calls=%fused_computation.249 | loop fusion | flops 294912 | bytes 1310720 | tf_op jit(solution)/shard_map/add | solution.py:52
  2.7 0.0 copy-start.6
  2.7 0.0 copy-start.7
  2.8 3.1 %gather_fusion = f32[512]{0:T(512)S(1)} fusion(f32[16384]{0:T(1024)S(1)} %bitcast_add_fusion, s32[1024]{0:T(1024)S(1)} %pad_clamp_fusion), kind=kCustom, calls=%fused_computation | custom fusion | bytes 6144 | tf_op jit(solution)/shard_map/gather | solution.py:113
  6.0 0.1 select_reduce_fusion
  6.1 8.3 %psum.14 = f32[40]{0:T(128)S(1)} all-reduce(f32[40]{0:T(128)S(1)} %select_reduce_fusion), channel_id=1, replica_groups=mesh['gx'=8,'gy'=2,'gz'=2] {'gy','gz'}, use_global_device_ids=true, to_apply=%region_1.2 | all-reduce | flops 40 | bytes 320 | tf_op jit(solution)/shard_map/psum | solution.py:120
  14.4 21.7 %psum.15 = f32[40]{0:T(128)S(1)} all-reduce(f32[40]{0:T(128)S(1)} %psum.14), channel_id=1, replica_groups=mesh['gx'=8,'gy'=2,'gz'=2] {'gx'}, use_global_device_ids=true, to_apply=%region_2.3 | all-reduce | flops 40 | bytes 320 | tf_op jit(solution)/shard_map/psum | solution.py:120
  36.1 0.1 select_reduce_fusion.1
  36.2 0.0 copy-start.8
  36.2 0.1 fusion.168
  36.3 3.3 %scatter_custom_fusion = f32[16384]{0:T(1024)S(1)} fusion(s32[512]{0:T(512)S(1)} %bitcast.409, f32[512]{0:T(512)S(1)} %multiply_select_fusion, f32[]{:T(128)} %constant.4.clone.1), kind=kCustom, calls=%fused_computation.305 | custom fusion | flops 512 | bytes 65540 | tf_op jit(solution)/shard_map/scatter-add | solution.py:129
  39.6 0.2 fusion.1
  39.8 0.1 copy.82
  40.9 0.2 fusion.175
  41.1 0.1 collective-permute-start
  41.2 4.7 %collective-permute-start.1 = (f32[19,16,1,128]{3,1,2,0:T(8,128)S(1)}, f32[19,16,1,128]{3,1,2,0:T(8,128)S(1)}, u32[]{:S(2)}, u32[]{:S(2)}) collective-permute-start(f32[19,16,1,128]{3,1,2,0:T(8,128)S(1)} %bitcast.404), channel_id=1, source_target_pairs={{4,0},{8,4},{12,8},{16,12},{20,16},{24,20},{28,24},{0,28},{5,1},{9... | collective-permute-start | bytes 466952 | tf_op jit(solution)/shard_map/ppermute | solution.py:44
  45.9 3.2 %collective-permute-done = f32[19,16,1,128]{3,1,2,0:T(8,128)S(1)} collective-permute-done((f32[19,16,1,128]{3,1,2,0:T(8,128)S(1)}, f32[19,16,1,128]{3,1,2,0:T(8,128)S(1)}, u32[]{:S(2)}, u32[]{:S(2)}) %collective-permute-start) | collective-permute-done | bytes 155680 | tf_op jit(solution)/shard_map/ppermute | solution.py:41
  49.1 1.0 %copy-done.3 = f32[19,16,8,128]{3,2,1,0:T(8,128)} copy-done((f32[19,16,8,128]{3,2,1,0:T(8,128)}, f32[19,16,8,128]{3,2,1,0:T(8,128)S(1)}, u32[]{:S(2)}) %copy-start.3) | copy-done | bytes 1245208
  50.1 0.5 pad_maximum_fusion
  50.6 3.1 %fusion.174 = (f32[19,16,10,1]{3,2,1,0:T(8,128)}, f32[19,16,10,1]{3,2,1,0:T(8,128)}) fusion(f32[19,16,10,128]{3,2,1,0:T(8,128)S(1)} %pad_maximum_fusion), kind=kLoop, calls=%fused_computation.315 | loop fusion | bytes 48640 | tf_op jit(solution)/shard_map/slice | solution.py:44
  53.7 2.8 %copy.56 = f32[19,16,10,1]{0,1,3,2:T(8,128)S(1)} copy(f32[19,16,10,1]{3,2,1,0:T(8,128)} %get-tuple-element.18) | data formatting | bytes 24320 | tf_op jit(solution)/shard_map/slice | solution.py:42
  56.5 0.5 collective-permute-start.2
  57.1 0.6 constant_dynamic-update-slice_fusion.35
  57.7 2.8 %copy.58 = f32[19,16,10,1]{0,1,3,2:T(8,128)S(1)} copy(f32[19,16,10,1]{3,2,1,0:T(8,128)} %get-tuple-element.17) | data formatting | bytes 24320 | tf_op jit(solution)/shard_map/slice | solution.py:44
  60.5 1.6 %collective-permute-start.3 = (f32[19,16,10,1]{0,1,3,2:T(8,128)S(1)}, f32[19,16,10,1]{0,1,3,2:T(8,128)S(1)}, u32[]{:S(2)}, u32[]{:S(2)}) collective-permute-start(f32[19,16,10,1]{0,1,3,2:T(8,128)S(1)} %copy.58), channel_id=1, source_target_pairs={{2,0},{0,2},{3,1},{1,3},{6,4},{4,6},{7,5},{5,7},{10,8},{8,10},{11,... | collective-permute-start | bytes 36488 | tf_op jit(solution)/shard_map/ppermute | solution.py:44
  62.1 3.7 %copy.57 = f32[19,16,10,1]{3,2,1,0:T(8,128)} copy(f32[19,16,10,1]{0,1,3,2:T(8,128)S(1)} %collective-permute-done.2) | data formatting | bytes 24320 | tf_op jit(solution)/shard_map/ppermute | solution.py:41
  65.8 1.6 %constant_dynamic-update-slice_fusion.34 = f32[19,16,8,128]{3,2,1,0:T(8,128)} fusion(f32[19,16,8,128]{3,2,1,0:T(8,128)} %constant_dynamic-update-slice_fusion.35, f32[19,16,10,1]{3,2,1,0:T(8,128)} %copy.57, f32[19,16,1,128]{3,2,1,0:T(1,128)S(1)} %bitcast.387, f32[19,16,8,128]{3,2,1,0:T(8,128)S(1)} %constant_dynamic-update-slice_fusion, ...), kind=kLoop, calls=%fused_computation.63 | loop fusion | flops 49152 | bytes 4112384
  67.4 3.7 %copy.59 = f32[19,16,10,1]{3,2,1,0:T(8,128)} copy(f32[19,16,10,1]{0,1,3,2:T(8,128)S(1)} %collective-permute-done.3) | data formatting | bytes 24320 | tf_op jit(solution)/shard_map/ppermute | solution.py:44
  71.1 1.8 %pad_maximum_fusion.1 = (f32[19,1,10,130]{3,2,1,0:T(8,128)S(1)}, f32[19,1,10,130]{3,2,1,0:T(8,128)S(1)}) fusion(f32[19,16,10,1]{3,2,1,0:T(8,128)} %copy.59, f32[19,16,10,1]{3,2,1,0:T(8,128)} %copy.57, f32[19,16,1,128]{3,2,1,0:T(1,128)S(1)} %bitcast.388, f32[19,16,8,128]{3,2,1,0:T(8,128)S(1)} %constant_dynamic-update-slice_fusion, ...), kind=kLoop, calls=%fused_computation.3 | loop fusion | flops 197600 | bytes 1778400 | tf_op jit(solution)/shard_map/concatenate | solution.py:45
  72.9 0.1 collective-permute-start.5
  73.0 0.5 collective-permute-start.4
  73.5 0.8 constant_dynamic-update-slice_fusion.33
  74.2 0.8 collective-permute-done.4
  75.0 0.7 constant_dynamic-update-slice_fusion.32
  75.8 0.7 constant_dynamic-update-slice_fusion.31
  76.5 0.7 constant_dynamic-update-slice_fusion.30
  77.2 0.8 constant_dynamic-update-slice_fusion.29
  78.0 0.8 constant_dynamic-update-slice_fusion.28
  78.7 0.8 constant_dynamic-update-slice_fusion.27
  79.5 0.7 constant_dynamic-update-slice_fusion.26
  80.2 0.7 constant_dynamic-update-slice_fusion.25
  80.9 0.7 constant_dynamic-update-slice_fusion.24
  81.6 0.7 constant_dynamic-update-slice_fusion.23
  82.4 0.7 constant_dynamic-update-slice_fusion.22
  83.1 0.8 constant_dynamic-update-slice_fusion.21
  83.9 0.7 constant_dynamic-update-slice_fusion.20
  84.6 0.8 constant_dynamic-update-slice_fusion.19
  (48 shorter events, 0.9 us)
Async XLA Ops:
  2.7 3.2 %copy-start.6 = (s32[1,1,1,512]{3,2,1,0:T(1,128)S(1)}, s32[1,1,1,512]{3,2,1,0:T(1,128)}, u32[]{:S(2)}) copy-start(s32[1,1,1,512]{3,2,1,0:T(1,128)} %param.11) | copy-start | bytes 6148
  2.7 3.2 %copy-start.7 = (f32[1,1,1,512]{3,2,1,0:T(1,128)S(1)}, f32[1,1,1,512]{3,2,1,0:T(1,128)}, u32[]{:S(2)}) copy-start(f32[1,1,1,512]{3,2,1,0:T(1,128)} %param.12) | copy-start | bytes 6148
  2.7 33.4 %copy-start.9 = (s32[40]{0:T(128)S(1)}, s32[40]{0:T(128)}, u32[]{:S(2)}) copy-start(s32[40]{0:T(128)} %param.14) | copy-start | bytes 484
  2.7 33.5 %copy-start.10 = (f32[12]{0:T(128)S(1)}, f32[12]{0:T(128)}, u32[]{:S(2)}) copy-start(f32[12]{0:T(128)} %param.15) | copy-start | bytes 148
  2.7 33.5 %copy-start.5 = (f32[1,1,1,12,512]{4,2,3,1,0:T(1,128)S(1)}, f32[1,1,1,12,512]{4,2,3,1,0:T(1,128)}, u32[]{:S(2)}) copy-start(f32[1,1,1,12,512]{4,2,3,1,0:T(1,128)} %param.13) | copy-start | bytes 73732
  2.8 36.9 %copy-start.2 = (f32[19,16,8,128]{3,2,1,0:T(8,128)S(1)}, f32[19,16,8,128]{3,2,1,0:T(8,128)}, u32[]{:S(2)}) copy-start(f32[19,16,8,128]{3,2,1,0:T(8,128)} %param.8) | copy-start | bytes 3735556
  2.8 36.9 %copy-start.4 = (s32[16,8,128]{2,1,0:T(8,128)S(1)}, s32[16,8,128]{2,1,0:T(8,128)}, u32[]{:S(2)}) copy-start(s32[16,8,128]{2,1,0:T(8,128)} %param.9) | copy-start | bytes 196612
  36.1 3.9 %copy-start.11 = (f32[40]{0:T(128)}, f32[40]{0:T(128)S(1)}, u32[]{:S(2)}) copy-start(f32[40]{0:T(128)S(1)} %psum.15) | copy-start | bytes 484
  36.2 3.7 %copy-start.8 = (f32[12]{0:T(128)}, f32[12]{0:T(128)S(1)}, u32[]{:S(2)}) copy-start(f32[12]{0:T(128)S(1)} %mul.413) | copy-start | bytes 148
  41.1 8.0 %collective-permute-start = (f32[19,16,1,128]{3,1,2,0:T(8,128)S(1)}, f32[19,16,1,128]{3,1,2,0:T(8,128)S(1)}, u32[]{:S(2)}, u32[]{:S(2)}) collective-permute-start(f32[19,16,1,128]{3,1,2,0:T(8,128)S(1)} %bitcast.405), channel_id=1, source_target_pairs={{0,4},{4,8},{8,12},{12,16},{16,20},{20,24},{24,28},{28,0},{1,5},{5... | collective-permute-start | bytes 466952 | tf_op jit(solution)/shard_map/ppermute | solution.py:41
  41.2 7.9 %collective-permute-start.1 = (f32[19,16,1,128]{3,1,2,0:T(8,128)S(1)}, f32[19,16,1,128]{3,1,2,0:T(8,128)S(1)}, u32[]{:S(2)}, u32[]{:S(2)}) collective-permute-start(f32[19,16,1,128]{3,1,2,0:T(8,128)S(1)} %bitcast.404), channel_id=1, source_target_pairs={{4,0},{8,4},{12,8},{16,12},{20,16},{24,20},{28,24},{0,28},{5,1},{9... | collective-permute-start | bytes 466952 | tf_op jit(solution)/shard_map/ppermute | solution.py:44
  49.1 1.0 %copy-start.3 = (f32[19,16,8,128]{3,2,1,0:T(8,128)}, f32[19,16,8,128]{3,2,1,0:T(8,128)S(1)}, u32[]{:S(2)}) copy-start(f32[19,16,8,128]{3,2,1,0:T(8,128)S(1)} %constant_dynamic-update-slice_fusion.36) | copy-start | bytes 3735556
  56.5 5.6 %collective-permute-start.2 = (f32[19,16,10,1]{0,1,3,2:T(8,128)S(1)}, f32[19,16,10,1]{0,1,3,2:T(8,128)S(1)}, u32[]{:S(2)}, u32[]{:S(2)}) collective-permute-start(f32[19,16,10,1]{0,1,3,2:T(8,128)S(1)} %copy.56), channel_id=1, source_target_pairs={{0,2},{2,0},{1,3},{3,1},{4,6},{6,4},{5,7},{7,5},{8,10},{10,8},{9,1... | collective-permute-start | bytes 36488 | tf_op jit(solution)/shard_map/ppermute | solution.py:41
  60.5 6.9 %collective-permute-start.3 = (f32[19,16,10,1]{0,1,3,2:T(8,128)S(1)}, f32[19,16,10,1]{0,1,3,2:T(8,128)S(1)}, u32[]{:S(2)}, u32[]{:S(2)}) collective-permute-start(f32[19,16,10,1]{0,1,3,2:T(8,128)S(1)} %copy.58), channel_id=1, source_target_pairs={{2,0},{0,2},{3,1},{1,3},{6,4},{4,6},{7,5},{5,7},{10,8},{8,10},{11,... | collective-permute-start | bytes 36488 | tf_op jit(solution)/shard_map/ppermute | solution.py:44
  71.1 2.4 %copy-start.1 = (f32[19,16,10,1]{3,2,1,0:T(8,128)S(1)}, f32[19,16,10,1]{3,2,1,0:T(8,128)}, u32[]{:S(2)}) copy-start(f32[19,16,10,1]{3,2,1,0:T(8,128)} %copy.59) | copy-start | bytes 36484
  72.9 2.8 %collective-permute-start.5 = (f32[19,1,10,130]{3,2,1,0:T(8,128)S(1)}, f32[19,1,10,130]{3,2,1,0:T(8,128)S(1)}, u32[]{:S(2)}, u32[]{:S(2)}) collective-permute-start(f32[19,1,10,130]{3,2,1,0:T(8,128)S(1)} %get-tuple-element.15), channel_id=1, source_target_pairs={{1,0},{0,1},{3,2},{2,3},{5,4},{4,5},{7,6},{6,7},{9,8},{8,9},{11,10... | collective-permute-start | bytes 296408 | tf_op jit(solution)/shard_map/ppermute | solution.py:44
  73.0 2.0 %copy-start = (f32[19,16,10,1]{3,2,1,0:T(8,128)S(1)}, f32[19,16,10,1]{3,2,1,0:T(8,128)}, u32[]{:S(2)}) copy-start(f32[19,16,10,1]{3,2,1,0:T(8,128)} %copy.57) | copy-start | bytes 36484
  73.0 2.0 %collective-permute-start.4 = (f32[19,1,10,130]{3,2,1,0:T(8,128)S(1)}, f32[19,1,10,130]{3,2,1,0:T(8,128)S(1)}, u32[]{:S(2)}, u32[]{:S(2)}) collective-permute-start(f32[19,1,10,130]{3,2,1,0:T(8,128)S(1)} %get-tuple-element.16), channel_id=1, source_target_pairs={{0,1},{1,0},{2,3},{3,2},{4,5},{5,4},{6,7},{7,6},{8,9},{9,8},{10,11... | collective-permute-start | bytes 296408 | tf_op jit(solution)/shard_map/ppermute | solution.py:41
